TPU v7x, 256 devices: a whole 4x4x8 slice. The times are simulated.
256 devices in a mesh: seq: 16 (over y, z_lo, core), row: 4 (over z_hi), col: 4 (over x).
Axes of the slice: x: 4, y: 4, z: 8 (z_hi: 4, z_lo: 2; z = z_hi * 2 + z_lo), core: 2. Of those that a mesh axis runs over, the one named last changes fastest.
Arguments:
- tokens: bfloat16 [8192, 4096], P(('seq', 'row'), 'col'), may hold values from -6 to 6
- w_uvqk: bfloat16 [4096, 8192], P(('seq', 'row'), 'col'), may hold values from -0.09375 to 0.09375
- w_out: bfloat16 [2048, 4096], P('col', ('seq', 'row')), may hold values from -0.375 to 0.375
- rab_table: float32 [16, 32], replicated, may hold values from -4 to 4
- norm_gain: float32 [16, 128], replicated, may hold values from 0.5 to 2
- user_lengths: int32 [4], replicated, may hold values from 1 to 6144, 8192 in all
- bucket_ids: int32 [8192], P('seq'), may hold values from 0 to 8191, as said below
Outputs:
- layer_out: bfloat16 [8192, 4096], P(('seq', 'row'), 'col')
Inputs may be any that keep to these rules, and one draw needn't show every extreme that they name: bucket_ids never fall from one token to the next.
All inputs are finite; a program needn't handle non-finite values.
Results may differ from a plain program's by a relative error of at most 0.014.
Values may be sent and summed in bfloat16 or wider, within the bound.
No kernel may reach another device: no remote copies, remote signals or barrier semaphores. Data moves between devices by JAX's collectives and lax.ppermute only.
A program may use at most 64 MiB of HBM per device.

v0:
```python
import math
import jax
import jax.numpy as jnp
from jax import lax
from jax.sharding import PartitionSpec as P

DH = 128
NB = 32
norm_eps = 1e-05


def user_index(user_ends, positions):
    return jnp.sum((user_ends[None, :] <= positions[:, None]).astype(jnp.int32), axis=1)


def bucket_biases(table_rows, bucket_gap):
    one_hot = (bucket_gap[:, :, None] == jnp.arange(NB, dtype=jnp.int32)[None, None, :]).astype(
        jnp.float32
    )
    return jnp.einsum(
        "qkb,hb->hqk",
        one_hot,
        table_rows,
        precision=lax.Precision.HIGHEST,
        preferred_element_type=jnp.float32,
    )


def on_device(tokens, w_uvqk, w_out, rab_table, norm_gain, user_lengths, bucket_ids):
    feature_rows = lax.all_gather(tokens, "col", axis=1, tiled=True)
    local_rows = tokens.shape[0]
    width_cols = w_uvqk.shape[1]
    row_index = lax.axis_index("row")
    col_index = lax.axis_index("col")
    seq_index = lax.axis_index("seq")
    projected = jnp.dot(
        feature_rows,
        lax.all_gather(w_uvqk, ("seq", "row"), axis=0, tiled=True),
        preferred_element_type=jnp.float32,
    )
    local_heads = width_cols // (4 * DH)
    activated = jax.nn.silu(projected).astype(jnp.bfloat16).reshape(local_rows, local_heads, 4, DH)
    head_major = lax.all_to_all(activated, "row", split_axis=1, concat_axis=0, tiled=True)
    block_len = head_major.shape[0]
    per_device = head_major.shape[1]
    user_ends = jnp.cumsum(user_lengths)
    query_pos = seq_index * block_len + jnp.arange(block_len, dtype=jnp.int32)
    query_user = user_index(user_ends, query_pos)
    first_head = col_index * local_heads + row_index * per_device
    rab_rows = lax.dynamic_slice_in_dim(rab_table, first_head, per_device, 0)
    gain_rows = lax.dynamic_slice_in_dim(norm_gain, first_head, per_device, 0)
    queries = head_major[:, :, 2]
    key_value = head_major[:, :, 1:4:2]
    score_scale = DH ** (-0.5)
    running = jnp.zeros((block_len, per_device, DH), jnp.float32)
    kv_piece = lax.all_gather(key_value, "seq", axis=0, tiled=True)
    key_bucket = lax.all_gather(bucket_ids, "seq", axis=0, tiled=True)
    key_count = kv_piece.shape[0]
    sub_size = math.gcd(key_count, 256)
    sub_count = key_count // sub_size

    def sub_block(accum_in, sub_index):
        sub_first = sub_index * sub_size
        kv_sub = lax.dynamic_slice_in_dim(kv_piece, sub_first, sub_size, 0)
        bucket_sub = lax.dynamic_slice_in_dim(key_bucket, sub_first, sub_size, 0)
        key_pos = sub_first + jnp.arange(sub_size, dtype=jnp.int32)
        key_user = user_index(user_ends, key_pos)
        visible = (query_user[:, None] == key_user[None, :]) & (
            key_pos[None, :] <= query_pos[:, None]
        )
        bucket_gap = jnp.clip(bucket_ids[:, None] - bucket_sub[None, :], 0, NB - 1)
        biases = bucket_biases(rab_rows, bucket_gap)
        scores = (
            jnp.dot(queries[:, 0], kv_sub[:, 0, 1].T, preferred_element_type=jnp.float32)
            * score_scale
        )
        scores = scores + biases[0]
        weights = jnp.where(visible, jax.nn.silu(scores), jnp.float32(0.0)).astype(jnp.bfloat16)
        per_head = [jnp.dot(weights, kv_sub[:, 0, 0], preferred_element_type=jnp.float32)]
        accum_out = accum_in + jnp.stack(per_head, axis=1)
        return (accum_out, None)

    running, _ = lax.scan(sub_block, running, jnp.arange(sub_count, dtype=jnp.int32))
    head_mean = jnp.mean(running, axis=-1, keepdims=True)
    centered = running - head_mean
    head_var = jnp.mean(centered * centered, axis=-1, keepdims=True)
    normed = centered * lax.rsqrt(head_var + norm_eps) * gain_rows[None, :, :]
    gated = (normed * head_major[:, :, 0].astype(jnp.float32)).astype(jnp.bfloat16)
    token_major = lax.all_to_all(gated, "row", split_axis=0, concat_axis=1, tiled=True)
    gated_rows = token_major.reshape(local_rows, local_heads * DH)
    partials = jnp.dot(
        gated_rows,
        lax.all_gather(w_out, ("seq", "row"), axis=1, tiled=True),
        preferred_element_type=jnp.float32,
    )
    summed = lax.psum_scatter(
        partials.astype(jnp.bfloat16), "col", scatter_dimension=1, tiled=True
    ).astype(jnp.float32)
    return (tokens.astype(jnp.float32) + summed).astype(jnp.bfloat16)


def solution(mesh):
    placed = (
        P(("seq", "row"), "col"),
        P(("seq", "row"), "col"),
        P("col", ("seq", "row")),
        P(),
        P(),
        P(),
        P("seq"),
    )
    return jax.shard_map(
        on_device, mesh=mesh, in_specs=placed, out_specs=P(("seq", "row"), "col"), check_vma=False
    )
```

profile of v0, /device:TPU:8, one launch (start us, length us, event | category | flops | bytes accessed | tf_op | source)
XLA Modules:
  0.0 657.6 jit_solution(16882960967085766931)
XLA Ops:
  8.1 30.5 %all-gather.6.cloned.1.call-done = bf16[128,4096]{1,0:T(8,128)(2,1)} async-done(((bf16[128,1024]{1,0:T(8,128)(2,1)}), bf16[128,4096]{1,0:T(8,128)(2,1)}) %all-gather.6.cloned.1.call-update) | async-done | bytes 1048592 | tf_op jit(solution)/shard_map/all_gather | solution.py:30
  38.6 203.7 %all-gather.8.cloned.1.call-done = bf16[4096,2048]{1,0:T(8,128)(2,1)} async-done(((bf16[64,2048]{1,0:T(8,128)(2,1)}), bf16[4096,2048]{1,0:T(8,128)(2,1)}) %all-gather.8.cloned.1.call-update) | async-done | bytes 16777232 | tf_op jit(solution)/shard_map/all_gather | solution.py:38
  242.3 8.5 %multiply_convert_fusion = bf16[128,2048]{1,0:T(8,128)(2,1)S(1)} fusion(bf16[128,4096]{1,0:T(8,128)(2,1)} %all-gather.6.cloned.1.call-done, bf16[4096,2048]{1,0:T(8,128)(2,1)} %all-gather.8.cloned.1.call-done), kind=kOutput, calls=%fused_computation.33 | convolution fusion | flops 2148794368 | bytes 18350080 | tf_op jit(solution)/shard_map/dot_general | solution.py:36
  251.4 27.6 %all_to_all.33 = bf16[128,4,4,128]{3,2,0,1:T(4,128)(2,1)S(1)} all-to-all(bf16[128,4,4,128]{3,2,0,1:T(4,128)(2,1)S(1)} %copy.26), channel_id=1, replica_groups=mesh['seq'=16,'row'=4,'col'=4] {'row'}, dimensions={1} | all-to-all | bytes 1048576 | tf_op jit(solution)/shard_map/all_to_all | solution.py:43
  280.7 14.5 %all-gather = s32[16,1,512]{2,1,0:T(1,128)S(1)} all-gather(s32[1,1,512]{2,1,0:T(1,128)S(1)} %bitcast.80), channel_id=1, replica_groups=mesh['seq'=16,'row'=4,'col'=4] {'seq'}, dimensions={0}, use_global_device_ids=true | all-gather | bytes 34816 | tf_op jit(solution)/shard_map/all_gather | solution.py:57
  296.0 19.7 %all-gather.10.cloned.1.call-done = bf16[8192,1,2,128]{3,0,2,1:T(8,128)(2,1)} async-done(((bf16[512,1,2,128]{3,0,2,1:T(8,128)(2,1)}), bf16[8192,1,2,128]{3,0,2,1:T(8,128)(2,1)}) %all-gather.10.cloned.1.call-update) | async-done | bytes 4194320 | tf_op jit(solution)/shard_map/all_gather | solution.py:56
  315.8 289.0 %while.11 = (s32[]{:T(128)}, f32[512,1,128]{2,0,1:T(8,128)S(1)}, s32[512]{0:T(512)S(1)}, s32[4]{0:T(128)S(1)}, s32[32]{0:T(128)S(1)}, /*index=5*/bf16[8192,1,2,1...) while((s32[]{:T(128)}, f32[512,1,128]{2,0,1:T(8,128)S(1)}, ...), condition=%wide.region_4.5_spmd.clone, body=%wide.region_2.4_spmd.clone.sunk | while | flops 123473408 | bytes 3950976 | solution.py:83
  317.2 5.3 fusion.36
  326.3 5.3 fusion.36
  335.3 5.3 fusion.36
  344.3 5.3 fusion.36
  353.4 5.3 fusion.36
  362.4 5.3 fusion.36
  371.4 5.3 fusion.36
  380.5 5.3 fusion.36
  389.5 5.3 fusion.36
  398.5 5.3 fusion.36
  407.6 5.3 fusion.36
  416.6 5.3 fusion.36
  425.6 5.3 fusion.36
  434.6 5.3 fusion.36
  443.7 5.3 fusion.36
  452.7 5.3 fusion.36
  461.7 5.3 fusion.36
  470.8 5.3 fusion.36
  479.8 5.3 fusion.36
  488.8 5.3 fusion.36
  497.9 5.3 fusion.36
  506.9 5.3 fusion.36
  515.9 5.3 fusion.36
  606.6 15.3 %all_to_all.34 = bf16[4,2,8192]{2,1,0:T(2,128)(2,1)S(1)} all-to-all(bf16[4,2,8192]{2,1,0:T(2,128)(2,1)S(1)} %reshape.130), channel_id=1, replica_groups=mesh['seq'=16,'row'=4,'col'=4] {'row'}, dimensions={0} | all-to-all | bytes 262144 | tf_op jit(solution)/shard_map/all_to_all | solution.py:89
  627.0 22.4 %reduce-scatter.2.cloned.1.call-done = bf16[128,1024]{1,0:T(8,128)(2,1)} async-done(((bf16[128,4096]{1,0:T(8,128)(2,1)}), bf16[128,1024]{1,0:T(8,128)(2,1)}) %reduce-scatter.2.cloned.1.call-update) | async-done | bytes 262160 | tf_op jit(solution)/shard_map/reduce_scatter | solution.py:96
  (309 shorter events, 158.3 us)
Async XLA Ops:
  6.5 289.4 %copy-start = (f32[16,128]{1,0:T(8,128)S(1)}, f32[16,128]{1,0:T(8,128)}, u32[]{:S(2)}) copy-start(f32[16,128]{1,0:T(8,128)} %param.13) | copy-start | bytes 24580
  6.5 32.0 %all-gather.6.cloned.1.call-start = ((), (), s32[]{:S(2)}) async-start(), calls=%async_computation.3 | async-start | bytes 1310720 | tf_op jit(solution)/shard_map/all_gather | solution.py:30
  7.3 235.0 %all-gather.8.cloned.1.call-start = ((), (), s32[]{:S(2)}) async-start(), calls=%async_computation.4 | async-start | bytes 17039360 | tf_op jit(solution)/shard_map/all_gather | solution.py:38
  8.0 307.7 %all-gather.10.cloned.1.call-start = ((), (), s32[]{:S(2)}) async-start(), calls=%async_computation.5 | async-start | bytes 4456448 | tf_op jit(solution)/shard_map/all_gather | solution.py:56
  250.8 29.7 %copy-start.3 = (s32[4]{0:T(128)S(1)}, s32[4]{0:T(128)}, u32[]{:S(2)}) copy-start(s32[4]{0:T(128)} %param.14) | copy-start | bytes 52
  250.8 29.9 %copy-start.2 = (s32[512]{0:T(512)S(1)}, s32[512]{0:T(512)}, u32[]{:S(2)}) copy-start(s32[512]{0:T(512)} %param.15) | copy-start | bytes 6148
  279.9 342.4 %all-gather.12.cloned.1.call-start = ((), (), s32[]{:S(2)}) async-start(), calls=%async_computation.6 | async-start | bytes 4259840 | tf_op jit(solution)/shard_map/all_gather | solution.py:93
  280.5 368.9 %reduce-scatter.2.cloned.1.call-start = ((), (), s32[]{:S(2)}) async-start(), calls=%async_computation.7 | async-start | bytes 1310720 | tf_op jit(solution)/shard_map/reduce_scatter | solution.py:96
  605.4 44.0 %copy-start.1 = (bf16[128,1024]{1,0:T(8,128)(2,1)S(1)}, bf16[128,1024]{1,0:T(8,128)(2,1)}, u32[]{:S(2)}) copy-start(bf16[128,1024]{1,0:T(8,128)(2,1)} %param.9) | copy-start | bytes 786436
Sparse Core Ops, SparseCore 0:
  9.2 29.3 all-gather.5
  40.4 201.8 all-gather.7
  280.0 35.7 all-gather.9
  317.4 185.4 all-gather.11
  627.1 22.2 reduce-scatter.1
where the time goes:
time: 660 us; the launch traced here: 658 us
  waiting for transfers between devices  278 us (42%)
  matrix products  229 us (35%)
  blocking collectives  57.5 us (9%)
  local copies, waits for them, and re-layouts  45.7 us (7%)
  loops' own time  22.8 us (3%)
  between operations  13.3 us (2%)
  other arithmetic  11.2 us (2%)
    all_gather x1, waiting for transfers between devices, on_device(): lax.all_gather(w_uvqk, ('seq', 'row'), axis=0, tiled=True)  204 us
    dot_general x32, matrix products, bucket_biases(): jnp.einsum('qkb,hb->hqk', one_hot, table_rows, precision=lax.Precision.HI...  168 us
    dot_general x32, matrix products, sub_block(): jnp.dot(weights, kv_sub[:, 0, 0], preferred_element_type=jnp.float32)  47.3 us
    all_gather x1, waiting for transfers between devices, on_device(): feature_rows = lax.all_gather(tokens, 'col', axis=1, tiled=True)  30.5 us
    all_to_all x1, blocking collectives, on_device(): lax.all_to_all(activated, 'row', split_axis=1, concat_axis=0, tiled=True)  27.6 us
    another operation x1, loops' own time, on_device(): lax.scan(sub_block, running, jnp.arange(sub_count, dtype=jnp.int32))  22.8 us
    reduce_scatter x1, waiting for transfers between devices, on_device(): lax.psum_scatter(partials.astype(jnp.bfloat16), 'col', scatter_dimension=...  22.4 us
    dot_general x32, local copies, waits for them, and re-layouts, bucket_biases(): jnp.einsum('qkb,hb->hqk', one_hot, table_rows, precision=lax.Precision.HI...  21.5 us
  transfers between devices with their start and end apart: 5, of which 4 were waited for; matrix products, arithmetic and copies ran while one was open for 41% of the time, Pallas kernels for 0%

commit v1 on v0

--- a/solution.py
+++ b/solution.py
@@ -27,7 +27,26 @@
 
 
 def on_device(tokens, w_uvqk, w_out, rab_table, norm_gain, user_lengths, bucket_ids):
-    feature_rows = lax.all_gather(tokens, "col", axis=1, tiled=True)
+
+    def shapes_compute(array_in):
+        axis_name = "col"
+        n_blocks = jax.lax.axis_size(axis_name)
+        kk = 0
+        lanes = []
+        while kk < n_blocks:
+            lanes.append((kk, (kk + 1) % n_blocks))
+            kk += 1
+        block_out = [None] * n_blocks
+        block_out[n_blocks - 1] = array_in
+        for at in range(n_blocks - 2, -1, -1):
+            block_out[at] = jax.lax.ppermute(block_out[at + 1], axis_name=axis_name, perm=lanes)
+        all_values = jnp.concatenate(block_out, 1)
+        u_next = jax.lax.axis_index(axis_name)
+        f_next = (u_next + 1) * array_in.shape[1]
+        near = jnp.roll(all_values, f_next, 1)
+        return near
+
+    feature_rows = shapes_compute(tokens)
     local_rows = tokens.shape[0]
     width_cols = w_uvqk.shape[1]
     row_index = lax.axis_index("row")

time: 660 us -> 630 us (0.955)
  waiting for transfers between devices: 278 us -> 246 us
    all_gather x1 -> x0, waiting for transfers between devices: 30.5 us -> none  [on_device(): feature_rows = lax.all_gather(tokens, 'col', axis=1, tiled=True)]
    all_gather x1, waiting for transfers between devices: 204 us -> 180 us  [on_device(): lax.all_gather(w_uvqk, ('seq', 'row'), axis=0, tiled=True)]
    ppermute x0 -> x3, waiting for transfers between devices: none -> 23.7 us  [shapes_compute(): jax.lax.ppermute(block_out[at + 1], axis_name=axis_name, perm=lanes)]
  transfers between devices with their start and end apart: 5 -> 7, of which waited for: 4 -> 6; matrix products, arithmetic and copies ran while one was open for 41% -> 43% of each run, Pallas kernels for 0% -> 0%
where the time goes in v1:
time: 630 us; the launch traced here: 628 us
  waiting for transfers between devices  246 us (39%)
  matrix products  228 us (36%)
  blocking collectives  57.8 us (9%)
  local copies, waits for them, and re-layouts  46.8 us (7%)
  loops' own time  22.8 us (4%)
  between operations  13.3 us (2%)
  other arithmetic  11.2 us (2%)
    all_gather x1, waiting for transfers between devices, on_device(): lax.all_gather(w_uvqk, ('seq', 'row'), axis=0, tiled=True)  180 us
    dot_general x32, matrix products, bucket_biases(): jnp.einsum('qkb,hb->hqk', one_hot, table_rows, precision=lax.Precision.HI...  168 us
    dot_general x32, matrix products, sub_block(): jnp.dot(weights, kv_sub[:, 0, 0], preferred_element_type=jnp.float32)  47.1 us
    all_to_all x1, blocking collectives, on_device(): lax.all_to_all(activated, 'row', split_axis=1, concat_axis=0, tiled=True)  27.6 us
    ppermute x3, waiting for transfers between devices, shapes_compute(): jax.lax.ppermute(block_out[at + 1], axis_name=axis_name, perm=lanes)  23.7 us
    another operation x1, loops' own time, on_device(): lax.scan(sub_block, running, jnp.arange(sub_count, dtype=jnp.int32))  22.8 us
    reduce_scatter x1, waiting for transfers between devices, on_device(): lax.psum_scatter(partials.astype(jnp.bfloat16), 'col', scatter_dimension=...  22 us
    dot_general x32, local copies, waits for them, and re-layouts, bucket_biases(): jnp.einsum('qkb,hb->hqk', one_hot, table_rows, precision=lax.Precision.HI...  21.5 us
  transfers between devices with their start and end apart: 7, of which 6 were waited for; matrix products, arithmetic and copies ran while one was open for 43% of the time, Pallas kernels for 0%

profile of v1, /device:TPU:8, one launch (start us, length us, event | category | flops | bytes accessed | tf_op | source)
XLA Modules:
  0.0 628.2 jit_solution(7569786832721845754)
XLA Ops:
  8.9 8.0 %collective-permute-done = bf16[128,1024]{1,0:T(8,128)(2,1)S(1)} collective-permute-done((bf16[128,1024]{1,0:T(8,128)(2,1)}, bf16[128,1024]{1,0:T(8,128)(2,1)S(1)}, u32[]{:S(2)}, u32[]{:S(2)}) %collective-permute-start) | collective-permute-done | bytes 262176 | tf_op jit(solution)/shard_map/ppermute | solution.py:42
  17.1 8.1 %collective-permute-done.1 = bf16[128,1024]{1,0:T(8,128)(2,1)S(1)} collective-permute-done((bf16[128,1024]{1,0:T(8,128)(2,1)S(1)}, bf16[128,1024]{1,0:T(8,128)(2,1)S(1)}, u32[]{:S(2)}, u32[]{:S(2)}) %collective-permute-start.1) | collective-permute-done | bytes 262176 | tf_op jit(solution)/shard_map/ppermute | solution.py:42
  25.2 7.6 %collective-permute-done.2 = bf16[128,1024]{1,0:T(8,128)(2,1)S(1)} collective-permute-done((bf16[128,1024]{1,0:T(8,128)(2,1)S(1)}, bf16[128,1024]{1,0:T(8,128)(2,1)S(1)}, u32[]{:S(2)}, u32[]{:S(2)}) %collective-permute-start.2) | collective-permute-done | bytes 262176 | tf_op jit(solution)/shard_map/ppermute | solution.py:42
  34.0 179.6 %all-gather.5.cloned.1.call-done = bf16[4096,2048]{1,0:T(8,128)(2,1)} async-done(((bf16[64,2048]{1,0:T(8,128)(2,1)}), bf16[4096,2048]{1,0:T(8,128)(2,1)}) %all-gather.5.cloned.1.call-update) | async-done | bytes 16777232 | tf_op jit(solution)/shard_map/all_gather | solution.py:57
  213.6 8.2 %multiply_convert_fusion = bf16[128,2048]{1,0:T(8,128)(2,1)S(1)} fusion(bf16[4096,2048]{1,0:T(8,128)(2,1)} %all-gather.5.cloned.1.call-done, bf16[128,8192]{1,0:T(8,128)(2,1)S(1)} %constant_dynamic-update-slice_fusion, s32[]{:T(128)S(6)} %select_n.26), kind=kOutput, calls=%fused_computation.33 | convolution fusion | flops 2148794368 | bytes 18350084 | tf_op jit(solution)/shard_map/dot_general | solution.py:55
  222.4 27.6 %all_to_all.33 = bf16[128,4,4,128]{3,2,0,1:T(4,128)(2,1)S(1)} all-to-all(bf16[128,4,4,128]{3,2,0,1:T(4,128)(2,1)S(1)} %copy.26), channel_id=1, replica_groups=mesh['seq'=16,'row'=4,'col'=4] {'row'}, dimensions={1} | all-to-all | bytes 1048576 | tf_op jit(solution)/shard_map/all_to_all | solution.py:62
  251.9 14.8 %all-gather = s32[16,1,512]{2,1,0:T(1,128)S(1)} all-gather(s32[1,1,512]{2,1,0:T(1,128)S(1)} %bitcast.79), channel_id=1, replica_groups=mesh['seq'=16,'row'=4,'col'=4] {'seq'}, dimensions={0}, use_global_device_ids=true | all-gather | bytes 34816 | tf_op jit(solution)/shard_map/all_gather | solution.py:76
  267.4 19.3 %all-gather.7.cloned.1.call-done = bf16[8192,1,2,128]{3,0,2,1:T(8,128)(2,1)} async-done(((bf16[512,1,2,128]{3,0,2,1:T(8,128)(2,1)}), bf16[8192,1,2,128]{3,0,2,1:T(8,128)(2,1)}) %all-gather.7.cloned.1.call-update) | async-done | bytes 4194320 | tf_op jit(solution)/shard_map/all_gather | solution.py:75
  286.7 288.9 %while.11 = (s32[]{:T(128)}, f32[512,1,128]{2,0,1:T(8,128)S(1)}, s32[512]{0:T(512)S(1)}, s32[4]{0:T(128)S(1)}, s32[32]{0:T(128)S(1)}, /*index=5*/bf16[8192,1,2,1...) while((s32[]{:T(128)}, f32[512,1,128]{2,0,1:T(8,128)S(1)}, ...), condition=%wide.region_4.5_spmd.clone, body=%wide.region_2.4_spmd.clone.sunk | while | flops 123473408 | bytes 3950976 | solution.py:102
  288.2 5.3 fusion.41
  297.3 5.3 fusion.41
  306.3 5.3 fusion.41
  315.3 5.3 fusion.41
  324.3 5.3 fusion.41
  333.4 5.3 fusion.41
  342.4 5.3 fusion.41
  351.4 5.3 fusion.41
  360.5 5.3 fusion.41
  369.5 5.3 fusion.41
  378.5 5.3 fusion.41
  387.5 5.3 fusion.41
  396.6 5.3 fusion.41
  405.6 5.3 fusion.41
  414.6 5.3 fusion.41
  423.7 5.3 fusion.41
  432.7 5.3 fusion.41
  441.7 5.3 fusion.41
  450.7 5.3 fusion.41
  459.8 5.3 fusion.41
  541.0 5.3 fusion.41
  577.5 15.4 %all_to_all.34 = bf16[4,2,8192]{2,1,0:T(2,128)(2,1)S(1)} all-to-all(bf16[4,2,8192]{2,1,0:T(2,128)(2,1)S(1)} %reshape.130), channel_id=1, replica_groups=mesh['seq'=16,'row'=4,'col'=4] {'row'}, dimensions={0} | all-to-all | bytes 262144 | tf_op jit(solution)/shard_map/all_to_all | solution.py:108
  597.9 22.0 %reduce-scatter.2.cloned.1.call-done = bf16[128,1024]{1,0:T(8,128)(2,1)} async-done(((bf16[128,4096]{1,0:T(8,128)(2,1)}), bf16[128,1024]{1,0:T(8,128)(2,1)}) %reduce-scatter.2.cloned.1.call-update) | async-done | bytes 262160 | tf_op jit(solution)/shard_map/reduce_scatter | solution.py:115
  (320 shorter events, 171.1 us)
Async XLA Ops:
  6.5 260.8 %copy-start = (f32[16,128]{1,0:T(8,128)S(1)}, f32[16,128]{1,0:T(8,128)}, u32[]{:S(2)}) copy-start(f32[16,128]{1,0:T(8,128)} %param.13) | copy-start | bytes 24580
  6.5 27.4 %copy-start.1 = (bf16[128,1024]{1,0:T(8,128)(2,1)S(1)}, bf16[128,1024]{1,0:T(8,128)(2,1)}, u32[]{:S(2)}) copy-start(bf16[128,1024]{1,0:T(8,128)(2,1)} %param.9) | copy-start | bytes 786436
  6.5 207.0 %all-gather.5.cloned.1.call-start = ((), (), s32[]{:S(2)}) async-start(), calls=%async_computation.3 | async-start | bytes 17039360 | tf_op jit(solution)/shard_map/all_gather | solution.py:57
  7.3 279.5 %all-gather.7.cloned.1.call-start = ((), (), s32[]{:S(2)}) async-start(), calls=%async_computation.4 | async-start | bytes 4456448 | tf_op jit(solution)/shard_map/all_gather | solution.py:75
  7.3 9.5 %collective-permute-start = (bf16[128,1024]{1,0:T(8,128)(2,1)}, bf16[128,1024]{1,0:T(8,128)(2,1)S(1)}, u32[]{:S(2)}, u32[]{:S(2)}) collective-permute-start(bf16[128,1024]{1,0:T(8,128)(2,1)} %param.9), channel_id=1, source_target_pairs={{0,1},{1,2},{2,3},{3,0},{4,5},{5,6},{6,7},{7,4},{8,9},{9,10},{10,1... | collective-permute-start | bytes 786440 | tf_op jit(solution)/shard_map/ppermute | solution.py:42
  16.9 8.4 %collective-permute-start.1 = (bf16[128,1024]{1,0:T(8,128)(2,1)S(1)}, bf16[128,1024]{1,0:T(8,128)(2,1)S(1)}, u32[]{:S(2)}, u32[]{:S(2)}) collective-permute-start(bf16[128,1024]{1,0:T(8,128)(2,1)S(1)} %collective-permute-done), channel_id=1, source_target_pairs={{0,1},{1,2},{2,3},{3,0},{4,5},{5,6},{6,7},{7,4},{8,9},{9,10},{10,1... | collective-permute-start | bytes 786440 | tf_op jit(solution)/shard_map/ppermute | solution.py:42
  25.2 7.6 %collective-permute-start.2 = (bf16[128,1024]{1,0:T(8,128)(2,1)S(1)}, bf16[128,1024]{1,0:T(8,128)(2,1)S(1)}, u32[]{:S(2)}, u32[]{:S(2)}) collective-permute-start(bf16[128,1024]{1,0:T(8,128)(2,1)S(1)} %collective-permute-done.1), channel_id=1, source_target_pairs={{0,1},{1,2},{2,3},{3,0},{4,5},{5,6},{6,7},{7,4},{8,9},{9,10},{10,1... | collective-permute-start | bytes 786440 | tf_op jit(solution)/shard_map/ppermute | solution.py:42
  222.1 29.5 %copy-start.3 = (s32[4]{0:T(128)S(1)}, s32[4]{0:T(128)}, u32[]{:S(2)}) copy-start(s32[4]{0:T(128)} %param.14) | copy-start | bytes 52
  222.2 29.7 %copy-start.2 = (s32[512]{0:T(512)S(1)}, s32[512]{0:T(512)}, u32[]{:S(2)}) copy-start(s32[512]{0:T(512)} %param.15) | copy-start | bytes 6148
  250.9 342.4 %all-gather.9.cloned.1.call-start = ((), (), s32[]{:S(2)}) async-start(), calls=%async_computation.5 | async-start | bytes 4259840 | tf_op jit(solution)/shard_map/all_gather | solution.py:112
  251.6 368.3 %reduce-scatter.2.cloned.1.call-start = ((), (), s32[]{:S(2)}) async-start(), calls=%async_computation.6 | async-start | bytes 1310720 | tf_op jit(solution)/shard_map/reduce_scatter | solution.py:115
Sparse Core Ops, SparseCore 0:
  9.2 204.3 all-gather.4
  251.0 35.7 all-gather.6
  288.6 185.4 all-gather.8
  598.0 21.8 reduce-scatter.1
